TPU v7x, 32 devices: a whole 2x2x4 slice. The times are simulated.
32 devices in a mesh: grp: 2 (over y), cpl: 4 (over z), mem: 4 (over x, core).
Axes of the slice: x: 2, y: 2, z: 4, core: 2. Of those that a mesh axis runs over, the one named last changes fastest.
Arguments:
- sources: bfloat16 [16, 128, 4, 720], P(('grp', 'cpl'), None, 'mem'), parts along dimension 0, may hold values from -6 to 6
- weights: bfloat16 [64, 8, 128, 128], P(('grp', 'cpl')), parts along dimension 0, may hold values from -0.375 to 0.375
- cover_source: int32 [64, 8], P(('grp', 'cpl')), parts along dimension 0, may hold values from 0 to 3, as said below
- cover_count: int32 [64], P(('grp', 'cpl')), parts along dimension 0, may hold values from 4 to 8
- send_pick: int32 [8, 4], P('grp'), parts along dimension 0, may hold values from 0 to 1
Outputs:
- remapped: bfloat16 [64, 128, 4, 720], P(('grp', 'cpl'), None, 'mem'), parts along dimension 0
- ens_mean: float32 [64, 128, 720], P(('grp', 'cpl'), 'mem'), parts along dimension 0
There are 2 independent parts, one for each index of `grp`. A program takes and returns all parts, laid end to end along the dimension named above; each array names one. Nothing has to cross between parts.
Inputs may be any that keep to these rules, and one draw needn't show every extreme that they name: `cover_source`: among the slots k < 4 of the targets of one coupler device, every component device is named at least once.
All inputs are finite; a program needn't handle non-finite values.
Results may differ from a plain program's by a relative error of at most 0.001.
Values may be sent and summed in bfloat16 or wider, within the bound.
A program may use at most 64 MiB of HBM per device.

v0:
```python
import jax
import jax.numpy as jnp
from jax import lax
from jax.sharding import PartitionSpec as P


def limit(high_sum, lower_bound, upper_bound):
    center = jnp.mean(high_sum, axis=1)
    top_value = jnp.max(high_sum, axis=1)
    bottom_value = jnp.min(high_sum, axis=1)
    rising = (upper_bound - center) / (top_value - center + 0.25)
    falling = (center - lower_bound) / (center - bottom_value + 0.25)
    factor = jnp.clip(jnp.minimum(rising, falling), 0.0, 1.0)
    return center[:, None] + factor[:, None] * (high_sum - center[:, None])


def remap_blocks(source_pool, block_index, weights, live_mask):
    target_count, slot_count = block_index.shape
    node_count = source_pool.shape[1]
    row_shape = source_pool.shape[2:]
    high_sum = jnp.zeros((target_count, node_count) + row_shape, jnp.float32)
    lower_bound = jnp.full((target_count,) + row_shape, jnp.inf, jnp.float32)
    upper_bound = jnp.full((target_count,) + row_shape, -jnp.inf, jnp.float32)
    for pair_index in range(slot_count):
        blocks = jnp.take(source_pool, block_index[:, pair_index], axis=0)
        live_now = live_mask[:, pair_index]
        masked = jnp.where(
            live_now[:, None, None], weights[:, pair_index], jnp.zeros((), weights.dtype)
        )
        high_sum = high_sum + jnp.einsum(
            "tij,tjmf->timf", masked, blocks, preferred_element_type=jnp.float32
        )
        lowest = jnp.min(blocks, axis=1).astype(jnp.float32)
        highest = jnp.max(blocks, axis=1).astype(jnp.float32)
        lower_bound = jnp.where(
            live_now[:, None, None], jnp.minimum(lower_bound, lowest), lower_bound
        )
        upper_bound = jnp.where(
            live_now[:, None, None], jnp.maximum(upper_bound, highest), upper_bound
        )
    return limit(high_sum, lower_bound, upper_bound)


def local(sources, weights, cover_source, cover_count, send_pick):
    device = lax.axis_index("cpl")
    slot_range = jnp.arange(weights.shape[1], dtype=jnp.int32)
    live_mask = slot_range[None, :] < cover_count[:, None]
    outgoing = lax.dynamic_index_in_dim(send_pick, device, 0, keepdims=False)
    send_buffer = jnp.take(sources, outgoing, axis=0)
    limited = remap_blocks(
        lax.all_to_all(send_buffer, "cpl", split_axis=0, concat_axis=0, tiled=True),
        cover_source,
        weights,
        live_mask,
    )
    remapped = limited.astype(jnp.bfloat16)
    member_total = jnp.sum(limited, axis=2)
    summed = lax.psum_scatter(member_total, "mem", scatter_dimension=1, tiled=True)
    ens_mean = summed / (limited.shape[2] * lax.axis_size("mem"))
    return (remapped, ens_mean)


def solution(mesh):
    placed = (
        P(("grp", "cpl"), None, "mem", None),
        P(("grp", "cpl"), None, None, None),
        P(("grp", "cpl"), None),
        P(("grp", "cpl")),
        P("grp", None),
    )
    return jax.shard_map(
        local,
        mesh=mesh,
        in_specs=placed,
        out_specs=(P(("grp", "cpl"), None, "mem", None), P(("grp", "cpl"), "mem", None)),
        check_vma=False,
    )
```

profile of v0, /device:TPU:0, one launch (start us, length us, event | category | flops | bytes accessed | tf_op | source)
XLA Modules:
  0.0 133.1 jit_solution(15865504704738375874)
XLA Ops:
  9.4 1.0 bitcast_select_fusion.8
  10.4 6.3 %all-to-all-start = ((bf16[4,128,1,720]{1,3,2,0:T(8,128)(2,1)}), bf16[4,128,1,720]{1,3,2,0:T(8,128)(2,1)S(1)}, u32[]{:S(2)}, u32[]{:S(2)}) async-start(bf16[4,128,1,720]{1,3,2,0:T(8,128)(2,1)} %bitcast_select_fusion.8), calls=%async_computation | async-start | bytes 1474560 | tf_op jit(solution)/shard_map/all_to_all | solution.py:51
  17.2 18.5 %all-to-all-done = bf16[4,128,1,720]{1,3,2,0:T(8,128)(2,1)S(1)} async-done(((bf16[4,128,1,720]{1,3,2,0:T(8,128)(2,1)}), bf16[4,128,1,720]{1,3,2,0:T(8,128)(2,1)S(1)}, u32[]{:S(2)}, u32[]{:S(2)}) %all-to-all-start) | async-done | bytes 737312 | tf_op jit(solution)/shard_map/all_to_all | solution.py:51
  35.7 1.8 %gather_fusion.8 = bf16[8,128,720]{1,2,0:T(8,128)(2,1)} fusion(bf16[4,128,720]{1,2,0:T(8,128)(2,1)S(1)} %bitcast.178, s32[1024]{0:T(1024)S(1)} %pad_clamp_fusion), kind=kCustom, calls=%fused_computation.7.clone | custom fusion | bytes 2949152 | tf_op jit(solution)/shard_map/jit(_take)/gather | solution.py:25
  37.6 0.8 gather_fusion.7
  38.4 1.9 %gather_fusion.6 = bf16[8,128,720]{1,2,0:T(8,128)(2,1)} fusion(bf16[4,128,720]{1,2,0:T(8,128)(2,1)S(1)} %bitcast.180, s32[1024]{0:T(1024)S(1)} %pad_clamp_fusion.2), kind=kCustom, calls=%fused_computation.5.clone | custom fusion | bytes 2949152 | tf_op jit(solution)/shard_map/jit(_take)/gather | solution.py:25
  40.3 1.9 %gather_fusion.5 = bf16[8,128,720]{1,2,0:T(8,128)(2,1)} fusion(bf16[4,128,720]{1,2,0:T(8,128)(2,1)S(1)} %bitcast.181, s32[1024]{0:T(1024)S(1)} %pad_clamp_fusion.3), kind=kCustom, calls=%fused_computation.4.clone | custom fusion | bytes 2949152 | tf_op jit(solution)/shard_map/jit(_take)/gather | solution.py:25
  42.1 1.9 %gather_fusion.4 = bf16[8,128,720]{1,2,0:T(8,128)(2,1)} fusion(bf16[4,128,720]{1,2,0:T(8,128)(2,1)S(1)} %bitcast.182, s32[1024]{0:T(1024)S(1)} %pad_clamp_fusion.4), kind=kCustom, calls=%fused_computation.3.clone | custom fusion | bytes 2949152 | tf_op jit(solution)/shard_map/jit(_take)/gather | solution.py:25
  44.0 1.9 %gather_fusion.3 = bf16[8,128,720]{1,2,0:T(8,128)(2,1)} fusion(bf16[4,128,720]{1,2,0:T(8,128)(2,1)S(1)} %bitcast.183, s32[1024]{0:T(1024)S(1)} %pad_clamp_fusion.5), kind=kCustom, calls=%fused_computation.2.clone | custom fusion | bytes 2949152 | tf_op jit(solution)/shard_map/jit(_take)/gather | solution.py:25
  45.9 1.9 %gather_fusion.2 = bf16[8,128,720]{1,2,0:T(8,128)(2,1)} fusion(bf16[4,128,720]{1,2,0:T(8,128)(2,1)S(1)} %bitcast.184, s32[1024]{0:T(1024)S(1)} %pad_clamp_fusion.6), kind=kCustom, calls=%fused_computation.1.clone | custom fusion | bytes 2949152 | tf_op jit(solution)/shard_map/jit(_take)/gather | solution.py:25
  47.8 1.9 %gather_fusion.1 = bf16[8,128,720]{1,2,0:T(8,128)(2,1)} fusion(bf16[4,128,720]{1,2,0:T(8,128)(2,1)S(1)} %bitcast.185, s32[1024]{0:T(1024)S(1)} %pad_clamp_fusion.7), kind=kCustom, calls=%fused_computation.clone | custom fusion | bytes 2949152 | tf_op jit(solution)/shard_map/jit(_take)/gather | solution.py:25
  49.7 2.6 %fusion.18 = (bf16[8,720]{1,0:T(8,128)(2,1)S(1)}, bf16[8,720]{1,0:T(8,128)(2,1)S(1)}) fusion(bf16[8,128,720]{1,2,0:T(8,128)(2,1)} %gather_fusion.2, pred[8]{0:T(512)(128)(4,1)S(1)} %get-tuple-element.59), kind=kLoop, calls=%fused_computation.39 | loop fusion | flops 2200320 | bytes 1497608 | tf_op jit(solution)/shard_map/reduce_max | solution.py:34
  52.3 1.1 fusion.16
  53.4 2.1 %fusion.13 = f32[8,128,720]{1,2,0:T(8,128)S(1)} fusion(bf16[8,128,720]{1,2,0:T(8,128)(2,1)S(1)} %copy-done.6, pred[8]{0:T(512)(128)(4,1)S(1)} %get-tuple-element.60, bf16[8,8,128,128]{3,2,1,0:T(8,128)(2,1)} %param.8, pred[8]{0:T(512)(128)(4,1)S(1)} %get-tuple-element.43), kind=kOutput, calls=%fused_computation.31 | convolution fusion | flops 189612032 | bytes 4685840 | tf_op jit(solution)/shard_map/tij,tjmf->timf/dot_general | solution.py:30
  55.5 1.0 fusion.11
  56.9 1.1 fusion.20
  57.9 1.0 fusion.9
  59.3 1.1 fusion.22
  60.4 1.0 fusion.7
  61.8 1.1 fusion.24
  62.8 2.8 %fusion.5 = f32[8,128,720]{1,2,0:T(8,128)} fusion(bf16[8,128,720]{1,2,0:T(8,128)(2,1)S(1)} %copy-done.2, pred[8]{0:T(512)(128)(4,1)S(1)} %get-tuple-element.56, bf16[8,8,128,128]{3,2,1,0:T(8,128)(2,1)S(1)} %copy-done.8, pred[8]{0:T(512)(128)(4,1)S(1)} %get-tuple-element.39), kind=kOutput, calls=%fused_computation.19 | convolution fusion | flops 189612032 | bytes 4686848 | tf_op jit(solution)/shard_map/tij,tjmf->timf/dot_general | solution.py:30
  65.6 1.1 fusion.26
  66.7 2.7 %fusion.3 = f32[8,128,720]{1,2,0:T(8,128)} fusion(bf16[8,128,720]{1,2,0:T(8,128)(2,1)S(1)} %copy-done.1, pred[8]{0:T(512)(128)(4,1)S(1)} %get-tuple-element.55, bf16[8,8,128,128]{3,2,1,0:T(8,128)(2,1)S(1)} %copy-done.8, pred[8]{0:T(512)(128)(4,1)S(1)} %get-tuple-element.38), kind=kOutput, calls=%fused_computation.16 | convolution fusion | flops 189612032 | bytes 4686848 | tf_op jit(solution)/shard_map/tij,tjmf->timf/dot_general | solution.py:30
  69.3 1.1 fusion.28
  70.4 2.6 %fusion.1 = f32[8,128,720]{1,2,0:T(8,128)} fusion(bf16[8,128,720]{1,2,0:T(8,128)(2,1)S(1)} %gather_fusion.7, pred[8]{0:T(512)(128)(4,1)S(1)} %get-tuple-element.54, bf16[8,8,128,128]{3,2,1,0:T(8,128)(2,1)S(1)} %copy-done.8, pred[8]{0:T(512)(128)(4,1)S(1)} %get-tuple-element.37), kind=kOutput, calls=%fused_computation.13 | convolution fusion | flops 189612032 | bytes 4686848 | tf_op jit(solution)/shard_map/tij,tjmf->timf/dot_general | solution.py:30
  73.1 1.1 fusion.30
  74.1 6.7 %fusion.78 = (f32[8,720]{1,0:T(8,128)S(1)}, f32[8,720]{1,0:T(8,128)S(1)}, f32[8,720]{1,0:T(8,128)S(1)}, f32[8,128,720]{1,2,0:T(8,128)S(1)}) fusion(bf16[8,128,720]{1,2,0:T(8,128)(2,1)S(1)} %copy-done.7, pred[8]{0:T(512)(128)(4,1)S(1)} %get-tuple-element.53, bf16[8,8,128,128]{3,2,1,0:T(8,128)(2,1)} %param.8, pred[8]{0:T(512)(128)(4,1)S(1)} %get-tuple-element.36, ...), kind=kOutput, calls=%fused_computation.169 | convolution fusion | flops 196967552 | bytes 25398800 | tf_op jit(solution)/shard_map/tij,tjmf->timf/dot_general | solution.py:30
  81.0 3.3 %convert_bitcast_fusion = (bf16[8,128,1,720]{1,3,2,0:T(8,128)(2,1)}, f32[8,128,720]{1,2,0:T(8,128)S(1)}) fusion(f32[8,128,720]{1,2,0:T(8,128)S(1)} %get-tuple-element.44, f32[8,720]{1,0:T(8,128)S(1)} %fusion.60, f32[8,720]{1,0:T(8,128)S(1)} %broadcast_multiply_fusion.1), kind=kLoop, calls=%fused_computation.34 | loop fusion | flops 2949120 | bytes 7418880
  84.3 2.5 %copy.23 = f32[8,128,720]{2,0,1:T(8,128)} copy(f32[8,128,720]{1,2,0:T(8,128)S(1)} %get-tuple-element.35) | data formatting | bytes 5898240 | tf_op jit(solution)/shard_map/add | solution.py:14
  86.8 37.2 %reduce-scatter.2.cloned.1.call-done = f32[8,32,720]{2,0,1:T(8,128)} async-done(((f32[8,128,720]{2,0,1:T(8,128)}), f32[8,32,720]{2,0,1:T(8,128)}) %reduce-scatter.2.cloned.1.call-update) | async-done | bytes 737296 | tf_op jit(solution)/shard_map/reduce_scatter | solution.py:58
  124.0 1.2 broadcast_multiply_fusion
  125.2 1.1 copy.25
  (49 shorter events, 3.8 us)
Async XLA Ops:
  7.2 1.5 %copy-start = (bf16[2,128,1,720]{1,3,2,0:T(8,128)(2,1)S(1)}, bf16[2,128,1,720]{1,3,2,0:T(8,128)(2,1)}, u32[]{:S(2)}) copy-start(bf16[2,128,1,720]{1,3,2,0:T(8,128)(2,1)} %param.7) | copy-start | bytes 1105924
  9.3 7.3 %copy-start.9 = (s32[8,8]{1,0:T(8,128)S(1)}, s32[8,8]{1,0:T(8,128)}, u32[]{:S(2)}) copy-start(s32[8,8]{1,0:T(8,128)} %param.9) | copy-start | bytes 772
  9.3 7.8 %copy-start.10 = (s32[8]{0:T(128)S(1)}, s32[8]{0:T(128)}, u32[]{:S(2)}) copy-start(s32[8]{0:T(128)} %param.10) | copy-start | bytes 100
  10.4 25.4 %all-to-all-start = ((bf16[4,128,1,720]{1,3,2,0:T(8,128)(2,1)}), bf16[4,128,1,720]{1,3,2,0:T(8,128)(2,1)S(1)}, u32[]{:S(2)}, u32[]{:S(2)}) async-start(bf16[4,128,1,720]{1,3,2,0:T(8,128)(2,1)} %bitcast_select_fusion.8), calls=%async_computation | async-start | bytes 1474560 | tf_op jit(solution)/shard_map/all_to_all | solution.py:51
  16.7 107.3 %reduce-scatter.2.cloned.1.call-start = ((), (), s32[]{:S(2)}) async-start(), calls=%async_computation.2 | async-start | bytes 3932160 | tf_op jit(solution)/shard_map/reduce_scatter | solution.py:58
  49.7 2.6 %copy-start.6 = (bf16[8,128,720]{1,2,0:T(8,128)(2,1)S(1)}, bf16[8,128,720]{1,2,0:T(8,128)(2,1)}, u32[]{:S(2)}) copy-start(bf16[8,128,720]{1,2,0:T(8,128)(2,1)} %gather_fusion.1) | copy-start | bytes 4423684
  53.3 2.1 %copy-start.5 = (bf16[8,128,720]{1,2,0:T(8,128)(2,1)S(1)}, bf16[8,128,720]{1,2,0:T(8,128)(2,1)}, u32[]{:S(2)}) copy-start(bf16[8,128,720]{1,2,0:T(8,128)(2,1)} %gather_fusion.2) | copy-start | bytes 4423684
  53.3 2.1 %copy-start.8 = (bf16[8,8,128,128]{3,2,1,0:T(8,128)(2,1)S(1)}, bf16[8,8,128,128]{3,2,1,0:T(8,128)(2,1)}, u32[]{:S(2)}) copy-start(bf16[8,8,128,128]{3,2,1,0:T(8,128)(2,1)} %param.8) | copy-start | bytes 6291460
  55.5 1.4 %copy-start.4 = (bf16[8,128,720]{1,2,0:T(8,128)(2,1)S(1)}, bf16[8,128,720]{1,2,0:T(8,128)(2,1)}, u32[]{:S(2)}) copy-start(bf16[8,128,720]{1,2,0:T(8,128)(2,1)} %gather_fusion.3) | copy-start | bytes 4423684
  57.9 1.4 %copy-start.3 = (bf16[8,128,720]{1,2,0:T(8,128)(2,1)S(1)}, bf16[8,128,720]{1,2,0:T(8,128)(2,1)}, u32[]{:S(2)}) copy-start(bf16[8,128,720]{1,2,0:T(8,128)(2,1)} %gather_fusion.4) | copy-start | bytes 4423684
  60.4 1.4 %copy-start.2 = (bf16[8,128,720]{1,2,0:T(8,128)(2,1)S(1)}, bf16[8,128,720]{1,2,0:T(8,128)(2,1)}, u32[]{:S(2)}) copy-start(bf16[8,128,720]{1,2,0:T(8,128)(2,1)} %gather_fusion.5) | copy-start | bytes 4423684
  62.8 2.8 %copy-start.1 = (bf16[8,128,720]{1,2,0:T(8,128)(2,1)S(1)}, bf16[8,128,720]{1,2,0:T(8,128)(2,1)}, u32[]{:S(2)}) copy-start(bf16[8,128,720]{1,2,0:T(8,128)(2,1)} %gather_fusion.6) | copy-start | bytes 4423684
  70.4 2.6 %copy-start.7 = (bf16[8,128,720]{1,2,0:T(8,128)(2,1)S(1)}, bf16[8,128,720]{1,2,0:T(8,128)(2,1)}, u32[]{:S(2)}) copy-start(bf16[8,128,720]{1,2,0:T(8,128)(2,1)} %gather_fusion.8) | copy-start | bytes 4423684
Sparse Core Ops, SparseCore 0:
  86.9 37.0 reduce-scatter.1
where the time goes:
time: 134 us; the launch traced here: 133 us
  waiting for transfers between devices  55.7 us (42%)
  matrix products  19.9 us (15%)
  local copies, waits for them, and re-layouts  19.6 us (15%)
  other arithmetic  17.2 us (13%)
  between operations  14.3 us (11%)
  starting transfers between devices  6.32 us (5%)
    reduce_scatter x1, waiting for transfers between devices, local(): lax.psum_scatter(member_total, 'mem', scatter_dimension=1, tiled=True)  37.2 us
    dot_general x8, matrix products, remap_blocks(): jnp.einsum('tij,tjmf->timf', masked, blocks, preferred_element_type=jnp.f...  19.9 us
    all_to_all x1, waiting for transfers between devices, local(): lax.all_to_all(send_buffer, 'cpl', split_axis=0, concat_axis=0, tiled=True)  18.5 us
    gather x8, local copies, waits for them, and re-layouts, remap_blocks(): blocks = jnp.take(source_pool, block_index[:, pair_index], axis=0)  14 us
    reduce_max x8, other arithmetic, remap_blocks(): highest = jnp.max(blocks, axis=1).astype(jnp.float32)  10.1 us
    all_to_all x1, starting transfers between devices, local(): lax.all_to_all(send_buffer, 'cpl', split_axis=0, concat_axis=0, tiled=True)  6.32 us
    unnamed x1, other arithmetic  3.29 us
  transfers between devices with their start and end apart: 2, of which 2 were waited for; matrix products, arithmetic and copies ran while one was open for 0% of the time, Pallas kernels for 0%

commit v1 on v0

v1 whole, which is shorter than its diff:
```python
import functools

import jax
import jax.numpy as jnp
from jax import lax
from jax.experimental import pallas as pl
from jax.experimental.pallas import tpu as pltpu
from jax.sharding import PartitionSpec as P

MESH = pl.DeviceIdType.MESH
WIDTH = 128
GROUP = 4


def kernel(
    n_cpl,
    n_mem,
    cover_source,
    cover_count,
    send_pick,
    sources,
    weights,
    remapped,
    ens_mean,
    outgoing,
    pool,
    flipped,
    low,
    high,
    held,
    *rest,
):
    stages = n_mem.bit_length() - 1
    totals = rest[:stages]
    landed = rest[stages : 2 * stages]
    pool_send, pool_recv, weight_sem = rest[2 * stages : 2 * stages + 3]
    stage_send = rest[2 * stages + 3 : 3 * stages + 3]
    stage_recv = rest[3 * stages + 3 : 4 * stages + 3]
    targets, slots, nodes, _ = weights.shape
    levels = sources.shape[1]
    pieces = pl.cdiv(levels, WIDTH)
    groups = targets // GROUP
    share = nodes // n_mem
    me = lax.axis_index("cpl")
    member = lax.axis_index("mem")
    bits = [lax.rem(lax.div(member, 1 << s), 2) for s in range(stages)]
    partners = [member + (1 - 2 * bits[s]) * (1 << s) for s in range(stages)]

    weight_copy = pltpu.make_async_copy(weights, held, weight_sem)
    weight_copy.start()

    barrier = pltpu.get_barrier_semaphore()

    @pl.loop(1, n_cpl)
    def _(distance):
        pl.semaphore_signal(
            barrier, inc=1, device_id={"cpl": lax.rem(me + distance, n_cpl)}, device_id_type=MESH
        )

    for s in range(stages):
        pl.semaphore_signal(barrier, inc=1, device_id={"mem": partners[s]}, device_id_type=MESH)

    def rows_of(piece):
        return piece * WIDTH, min(WIDTH, levels - piece * WIDTH)

    def pool_copy(piece, distance, slot):
        start, size = rows_of(piece)
        return pltpu.make_async_remote_copy(
            src_ref=outgoing.at[distance - 1, pl.ds(start, size)],
            dst_ref=pool.at[slot, pl.ds(start, size)],
            send_sem=pool_send.at[piece, distance - 1],
            recv_sem=pool_recv.at[piece, distance - 1],
            device_id={"cpl": lax.rem(me + distance, n_cpl)},
            device_id_type=MESH,
        )

    def fill(piece):
        start, size = rows_of(piece)

        @pl.loop(1, n_cpl)
        def _(distance):
            chosen = send_pick[me, lax.rem(me + distance, n_cpl)]
            outgoing[distance - 1, pl.ds(start, size)] = sources[chosen, pl.ds(start, size)]

    def send(piece):
        @pl.loop(1, n_cpl)
        def _(distance):
            pool_copy(piece, distance, me).start()

    fill(0)
    pl.semaphore_wait(barrier, n_cpl - 1 + stages)
    send(0)
    for piece in range(1, pieces):
        fill(piece)
        send(piece)

    own = send_pick[me, me]
    pool[me, pl.ds(0, levels)] = sources[own]
    if pieces * WIDTH > levels:
        tail = pieces * WIDTH - levels
        pool[:, pl.ds(levels, tail)] = jnp.zeros((n_cpl, tail, nodes), pool.dtype)
    flipped[n_cpl] = jnp.zeros(flipped.shape[1:], flipped.dtype)
    weight_copy.wait()

    def stage_copy(s, piece, group):
        spot = (piece, group) if s == 0 else (piece,)
        return pltpu.make_async_remote_copy(
            src_ref=totals[s].at[spot + (1 - bits[s],)],
            dst_ref=landed[s].at[spot],
            send_sem=stage_send[s].at[spot],
            recv_sem=stage_recv[s].at[spot],
            device_id={"mem": partners[s]},
            device_id_type=MESH,
        )

    def remap(piece, target):
        start, size = rows_of(piece)
        count = cover_count[target]
        first = cover_source[target, 0]
        terms, lowest, highest = [], [], []
        for k in range(slots):
            block = cover_source[target, k]
            live = k < count
            terms.append(flipped[jnp.where(live, block, n_cpl)])
            ranged = jnp.where(live, block, first)
            lowest.append(low[ranged])
            highest.append(high[ranged])
        left = jnp.concatenate([held[target, k] for k in range(slots)], axis=1)
        right = jnp.concatenate(terms, axis=0)
        summed = jnp.dot(left, right, preferred_element_type=jnp.float32)
        lower = functools.reduce(jnp.minimum, lowest)
        upper = functools.reduce(jnp.maximum, highest)
        center = jnp.sum(summed, axis=0, keepdims=True) * (1.0 / nodes)
        top = jnp.max(summed, axis=0, keepdims=True)
        bottom = jnp.min(summed, axis=0, keepdims=True)
        rising = (upper - center) / (top - center + 0.25)
        falling = (center - lower) / (center - bottom + 0.25)
        factor = jnp.clip(jnp.minimum(rising, falling), 0.0, 1.0)
        limited = center + factor * (summed - center)
        turned = limited.astype(jnp.bfloat16).T
        remapped[target, pl.ds(start, size)] = turned[:size]
        return limited

    def collect(piece):
        last = stages - 1
        start, size = rows_of(piece)
        stage_copy(last, piece, 0).wait_recv()
        total = totals[last][piece, bits[last], 0] + landed[last][piece, 0]
        ens_mean[:, :, pl.ds(start, size)] = (total * (1.0 / n_mem))[:, :, :size]

    for piece in range(pieces):
        start, size = rows_of(piece)

        @pl.loop(1, n_cpl)
        def _(distance):
            pool_copy(piece, distance, lax.rem(me - distance + n_cpl, n_cpl)).wait_recv()

        @pl.loop(0, n_cpl)
        def _(block):
            values = pool[block, pl.ds(piece * WIDTH, WIDTH)].T
            flipped[block] = values
            wide = values.astype(jnp.float32)
            low[block] = jnp.min(wide, axis=0, keepdims=True)
            high[block] = jnp.max(wide, axis=0, keepdims=True)

        @pl.loop(0, groups)
        def _(group):
            for one in range(GROUP):
                limited = remap(piece, group * GROUP + one)
                for q in range(n_mem):
                    totals[0][piece, group, q % 2, q // 2, one] = limited[q * share : (q + 1) * share]
            stage_copy(0, piece, group).start()

        for s in range(1, stages):
            parts = n_mem >> s
            if s == 1:
                for group in range(groups):
                    stage_copy(0, piece, group).wait_recv()
                    for q in range(parts):
                        totals[1][piece, q % 2, q // 2, pl.ds(group * GROUP, GROUP)] = (
                            totals[0][piece, group, bits[0], q] + landed[0][piece, group, q]
                        )
            else:
                stage_copy(s - 1, piece, 0).wait_recv()
                for q in range(parts):
                    totals[s][piece, q % 2, q // 2] = (
                        totals[s - 1][piece, bits[s - 1], q] + landed[s - 1][piece, q]
                    )
            stage_copy(s, piece, 0).start()
        if piece > 0:
            collect(piece - 1)
    collect(pieces - 1)

    for piece in range(pieces):

        @pl.loop(1, n_cpl)
        def _(distance):
            pool_copy(piece, distance, me).wait_send()

        for group in range(groups):
            stage_copy(0, piece, group).wait_send()
        for s in range(1, stages):
            stage_copy(s, piece, 0).wait_send()


def local(n_cpl, n_mem, sources, weights, cover_source, cover_count, send_pick):
    blocks, nodes, members, levels = sources.shape
    targets, slots = cover_source.shape
    pieces = pl.cdiv(levels, WIDTH)
    padded = pieces * WIDTH
    groups = targets // GROUP
    share = nodes // n_mem
    stages = n_mem.bit_length() - 1
    turned = jnp.transpose(sources, (0, 2, 3, 1)).reshape(blocks, levels, nodes)
    totals, landed, sems = [], [], []
    for s in range(stages):
        half = (n_mem >> s) // 2
        if s == 0:
            lead, depth = (pieces, groups), GROUP
        else:
            lead, depth = (pieces,), targets
        totals.append(pltpu.VMEM(lead + (2, half, depth, share, WIDTH), jnp.float32))
        landed.append(pltpu.VMEM(lead + (half, depth, share, WIDTH), jnp.float32))
        sems.append(pltpu.SemaphoreType.DMA(lead))
    vmem = pl.BlockSpec(memory_space=pltpu.VMEM)
    smem = pl.BlockSpec(memory_space=pltpu.SMEM)
    remapped, ens_mean = pl.pallas_call(
        functools.partial(kernel, n_cpl, n_mem),
        out_shape=(
            jax.ShapeDtypeStruct((targets, levels, nodes), jnp.bfloat16),
            jax.ShapeDtypeStruct((targets, share, levels), jnp.float32),
        ),
        in_specs=[smem, smem, smem, vmem, pl.BlockSpec(memory_space=pl.ANY)],
        out_specs=(vmem, vmem),
        scratch_shapes=[
            pltpu.VMEM((n_cpl - 1, levels, nodes), jnp.bfloat16),
            pltpu.VMEM((n_cpl, padded, nodes), jnp.bfloat16),
            pltpu.VMEM((n_cpl + 1, nodes, WIDTH), jnp.bfloat16),
            pltpu.VMEM((n_cpl, 1, WIDTH), jnp.float32),
            pltpu.VMEM((n_cpl, 1, WIDTH), jnp.float32),
            pltpu.VMEM((targets, slots, nodes, nodes), jnp.bfloat16),
            *totals,
            *landed,
            pltpu.SemaphoreType.DMA((pieces, n_cpl - 1)),
            pltpu.SemaphoreType.DMA((pieces, n_cpl - 1)),
            pltpu.SemaphoreType.DMA,
            *sems,
            *sems,
        ],
        compiler_params=pltpu.CompilerParams(
            collective_id=0, has_side_effects=True, vmem_limit_bytes=56 * 1024 * 1024
        ),
        cost_estimate=pl.CostEstimate(
            flops=2 * targets * slots * nodes * nodes * levels,
            bytes_accessed=weights.size * 2 + targets * levels * nodes * 4,
            transcendentals=0,
        ),
    )(cover_source, cover_count, send_pick, turned, weights)
    remapped = jnp.transpose(remapped.reshape(targets, members, levels, nodes), (0, 3, 1, 2))
    return remapped, ens_mean


def solution(mesh):
    placed = (
        P(("grp", "cpl"), None, "mem", None),
        P(("grp", "cpl"), None, None, None),
        P(("grp", "cpl"), None),
        P(("grp", "cpl")),
        P("grp", None),
    )
    return jax.shard_map(
        functools.partial(local, mesh.shape["cpl"], mesh.shape["mem"]),
        mesh=mesh,
        in_specs=placed,
        out_specs=(P(("grp", "cpl"), None, "mem", None), P(("grp", "cpl"), "mem", None)),
        check_vma=False,
    )
```

time: 134 us -> 42.4 us (0.32)
  waiting for transfers between devices: 55.7 us -> 0 us
  Pallas kernels: 0 us -> 37.5 us
  matrix products: 19.9 us -> 0 us
  other arithmetic: 17.2 us -> 0 us
  local copies, waits for them, and re-layouts: 19.6 us -> 3.53 us
  between operations: 14.3 us -> 0.65 us
  starting transfers between devices: 6.32 us -> 0 us
    pallas_call x0 -> x1, Pallas kernels: none -> 37.5 us  [local(): pl.pallas_call(functools.partial(kernel, n_cpl, n_mem), out_shape=(jax.Sh...]
    reduce_scatter x1 -> x0, waiting for transfers between devices: 37.2 us -> none  [local(): lax.psum_scatter(member_total, 'mem', scatter_dimension=1, tiled=True)]
    dot_general x8 -> x0, matrix products: 19.9 us -> none  [remap_blocks(): jnp.einsum('tij,tjmf->timf', masked, blocks, preferred_element_type=jnp.f...]
    all_to_all x1 -> x0, waiting for transfers between devices: 18.5 us -> none  [local(): lax.all_to_all(send_buffer, 'cpl', split_axis=0, concat_axis=0, tiled=True)]
    gather x9 -> x0, local copies, waits for them, and re-layouts: 14.6 us -> none  [the longest x8 14 us: remap_blocks(): blocks = jnp.take(source_pool, block_index[:, pair_index], axis=0)]
    reduce_max x8 -> x0, other arithmetic: 10.1 us -> none  [remap_blocks(): highest = jnp.max(blocks, axis=1).astype(jnp.float32)]
    all_to_all x1 -> x0, starting transfers between devices: 6.32 us -> none  [local(): lax.all_to_all(send_buffer, 'cpl', split_axis=0, concat_axis=0, tiled=True)]
    unnamed x1 -> x0, other arithmetic: 3.29 us -> none
  transfers between devices with their start and end apart: 2 -> 0, of which waited for: 2 -> 0; matrix products, arithmetic and copies ran while one was open for 0% -> 0% of each run, Pallas kernels for 0% -> 0%
where the time goes in v1:
time: 42.4 us; the launch traced here: 41.7 us
  Pallas kernels  37.5 us (88%)
  local copies, waits for them, and re-layouts  3.53 us (8%)
  between operations  0.65 us (2%)
    pallas_call x1, Pallas kernels, local(): pl.pallas_call(functools.partial(kernel, n_cpl, n_mem), out_shape=(jax.Sh...  37.5 us
    unnamed x4, local copies, waits for them, and re-layouts  3.53 us

profile of v1, /device:TPU:0, one launch (start us, length us, event | category | flops | bytes accessed | tf_op | source)
XLA Modules:
  0.0 41.7 jit_solution(1122215376279291158)
XLA Ops:
  0.6 37.5 %shard_map.68 = (bf16[8,720,128]{2,1,0:T(8,128)(2,1)}, f32[8,32,720]{2,1,0:T(8,128)}) custom-call(s32[8,8]{1,0:T(8,128)} %cover_source.1, s32[8]{0:T(128)} %cover_count.1, s32[4,4]{1,0:T(4,128)} %send_pick.1, bf16[2,720,128]{2,1,0:T(8,128)(2,1)} %bitcast.11, bf16[8,8,128,128]{3,2,1,0:T(8,128)(2,1)} %weights.1), custom_call_target="tpu_custom_call" | custom-call | flops 1509949440 | bytes 5046272 | tf_op jit(solution)/shard_map/pallas_call | solution.py:227
  38.1 0.0 copy-start
  38.2 2.7 %copy.11 = bf16[8,128,1,720]{1,3,2,0:T(8,128)(2,1)} copy(bf16[8,128,1,720]{1,3,2,0:T(8,128)(2,1)} %bitcast.10) | data formatting | bytes 2949120
  40.8 0.0 copy-done
  40.8 0.9 %copy.12 = f32[8,32,720]{2,1,0:T(8,128)} copy(f32[8,32,720]{2,1,0:T(8,128)S(1)} %copy-done) | data formatting | bytes 1474560
Async XLA Ops:
  38.1 2.7 %copy-start = (f32[8,32,720]{2,1,0:T(8,128)S(1)}, f32[8,32,720]{2,1,0:T(8,128)}, u32[]{:S(2)}) copy-start(f32[8,32,720]{2,1,0:T(8,128)} %get-tuple-element.11) | copy-start | bytes 2211844

commit v2 on v1

--- a/solution.py
+++ b/solution.py
@@ -9,6 +9,7 @@
 
 MESH = pl.DeviceIdType.MESH
 WIDTH = 128
+AHEAD = 2
 GROUP = 4
 
 
@@ -28,14 +29,16 @@
     low,
     high,
     held,
+    limited_out,
+    mean_out,
     *rest,
 ):
     stages = n_mem.bit_length() - 1
     totals = rest[:stages]
     landed = rest[stages : 2 * stages]
-    pool_send, pool_recv, weight_sem = rest[2 * stages : 2 * stages + 3]
-    stage_send = rest[2 * stages + 3 : 3 * stages + 3]
-    stage_recv = rest[3 * stages + 3 : 4 * stages + 3]
+    pool_send, pool_recv, weight_sem, limited_sem, mean_sem = rest[2 * stages : 2 * stages + 5]
+    stage_send = rest[2 * stages + 5 : 3 * stages + 5]
+    stage_recv = rest[3 * stages + 5 : 4 * stages + 5]
     targets, slots, nodes, _ = weights.shape
     levels = sources.shape[1]
     pieces = pl.cdiv(levels, WIDTH)
@@ -92,7 +95,8 @@
     send(0)
     for piece in range(1, pieces):
         fill(piece)
-        send(piece)
+        if piece < AHEAD:
+            send(piece)
 
     own = send_pick[me, me]
     pool[me, pl.ds(0, levels)] = sources[own]
@@ -103,7 +107,7 @@
     weight_copy.wait()
 
     def stage_copy(s, piece, group):
-        spot = (piece, group) if s == 0 else (piece,)
+        spot = (piece, group)
         return pltpu.make_async_remote_copy(
             src_ref=totals[s].at[spot + (1 - bits[s],)],
             dst_ref=landed[s].at[spot],
@@ -138,15 +142,35 @@
         factor = jnp.clip(jnp.minimum(rising, falling), 0.0, 1.0)
         limited = center + factor * (summed - center)
         turned = limited.astype(jnp.bfloat16).T
-        remapped[target, pl.ds(start, size)] = turned[:size]
+        limited_out[target, pl.ds(start, size)] = turned[:size]
         return limited
+
+    def limited_copy(piece):
+        start, size = rows_of(piece)
+        return pltpu.make_async_copy(
+            limited_out.at[:, pl.ds(start, size)],
+            remapped.at[:, pl.ds(start, size)],
+            limited_sem.at[piece],
+        )
+
+    def mean_copy(piece):
+        start, size = rows_of(piece)
+        return pltpu.make_async_copy(
+            mean_out.at[:, :, pl.ds(start, size)],
+            ens_mean.at[:, :, pl.ds(start, size)],
+            mean_sem.at[piece],
+        )
 
     def collect(piece):
         last = stages - 1
         start, size = rows_of(piece)
-        stage_copy(last, piece, 0).wait_recv()
-        total = totals[last][piece, bits[last], 0] + landed[last][piece, 0]
-        ens_mean[:, :, pl.ds(start, size)] = (total * (1.0 / n_mem))[:, :, :size]
+        for group in range(groups):
+            stage_copy(last, piece, group).wait_recv()
+            total = totals[last][piece, group, bits[last], 0] + landed[last][piece, group, 0]
+            mean_out[pl.ds(group * GROUP, GROUP), :, pl.ds(start, size)] = (
+                total * (1.0 / n_mem)
+            )[:, :, :size]
+        mean_copy(piece).start()
 
     for piece in range(pieces):
         start, size = rows_of(piece)
@@ -154,6 +178,9 @@
         @pl.loop(1, n_cpl)
         def _(distance):
             pool_copy(piece, distance, lax.rem(me - distance + n_cpl, n_cpl)).wait_recv()
+
+        if piece + AHEAD < pieces:
+            send(piece + AHEAD)
 
         @pl.loop(0, n_cpl)
         def _(block):
@@ -171,22 +198,15 @@
                     totals[0][piece, group, q % 2, q // 2, one] = limited[q * share : (q + 1) * share]
             stage_copy(0, piece, group).start()
 
+        limited_copy(piece).start()
         for s in range(1, stages):
-            parts = n_mem >> s
-            if s == 1:
-                for group in range(groups):
-                    stage_copy(0, piece, group).wait_recv()
-                    for q in range(parts):
-                        totals[1][piece, q % 2, q // 2, pl.ds(group * GROUP, GROUP)] = (
-                            totals[0][piece, group, bits[0], q] + landed[0][piece, group, q]
-                        )
-            else:
-                stage_copy(s - 1, piece, 0).wait_recv()
-                for q in range(parts):
-                    totals[s][piece, q % 2, q // 2] = (
-                        totals[s - 1][piece, bits[s - 1], q] + landed[s - 1][piece, q]
+            for group in range(groups):
+                stage_copy(s - 1, piece, group).wait_recv()
+                for q in range(n_mem >> s):
+                    totals[s][piece, group, q % 2, q // 2] = (
+                        totals[s - 1][piece, group, bits[s - 1], q] + landed[s - 1][piece, group, q]
                     )
-            stage_copy(s, piece, 0).start()
+                stage_copy(s, piece, group).start()
         if piece > 0:
             collect(piece - 1)
     collect(pieces - 1)
@@ -198,9 +218,10 @@
             pool_copy(piece, distance, me).wait_send()
 
         for group in range(groups):
-            stage_copy(0, piece, group).wait_send()
-        for s in range(1, stages):
-            stage_copy(s, piece, 0).wait_send()
+            for s in range(stages):
+                stage_copy(s, piece, group).wait_send()
+        limited_copy(piece).wait()
+        mean_copy(piece).wait()
 
 
 def local(n_cpl, n_mem, sources, weights, cover_source, cover_count, send_pick):
@@ -215,14 +236,12 @@
     totals, landed, sems = [], [], []
     for s in range(stages):
         half = (n_mem >> s) // 2
-        if s == 0:
-            lead, depth = (pieces, groups), GROUP
-        else:
-            lead, depth = (pieces,), targets
-        totals.append(pltpu.VMEM(lead + (2, half, depth, share, WIDTH), jnp.float32))
-        landed.append(pltpu.VMEM(lead + (half, depth, share, WIDTH), jnp.float32))
+        lead = (pieces, groups)
+        totals.append(pltpu.VMEM(lead + (2, half, GROUP, share, WIDTH), jnp.float32))
+        landed.append(pltpu.VMEM(lead + (half, GROUP, share, WIDTH), jnp.float32))
         sems.append(pltpu.SemaphoreType.DMA(lead))
     vmem = pl.BlockSpec(memory_space=pltpu.VMEM)
+    whole = pl.BlockSpec(memory_space=pl.ANY)
     smem = pl.BlockSpec(memory_space=pltpu.SMEM)
     remapped, ens_mean = pl.pallas_call(
         functools.partial(kernel, n_cpl, n_mem),
@@ -230,8 +249,8 @@
             jax.ShapeDtypeStruct((targets, levels, nodes), jnp.bfloat16),
             jax.ShapeDtypeStruct((targets, share, levels), jnp.float32),
         ),
-        in_specs=[smem, smem, smem, vmem, pl.BlockSpec(memory_space=pl.ANY)],
-        out_specs=(vmem, vmem),
+        in_specs=[smem, smem, smem, vmem, pl.BlockSpec(memory_space=pltpu.HBM)],
+        out_specs=(whole, whole),
         scratch_shapes=[
             pltpu.VMEM((n_cpl - 1, levels, nodes), jnp.bfloat16),
             pltpu.VMEM((n_cpl, padded, nodes), jnp.bfloat16),
@@ -239,16 +258,20 @@
             pltpu.VMEM((n_cpl, 1, WIDTH), jnp.float32),
             pltpu.VMEM((n_cpl, 1, WIDTH), jnp.float32),
             pltpu.VMEM((targets, slots, nodes, nodes), jnp.bfloat16),
+            pltpu.VMEM((targets, levels, nodes), jnp.bfloat16),
+            pltpu.VMEM((targets, share, levels), jnp.float32),
             *totals,
             *landed,
             pltpu.SemaphoreType.DMA((pieces, n_cpl - 1)),
             pltpu.SemaphoreType.DMA((pieces, n_cpl - 1)),
             pltpu.SemaphoreType.DMA,
+            pltpu.SemaphoreType.DMA((pieces,)),
+            pltpu.SemaphoreType.DMA((pieces,)),
             *sems,
             *sems,
         ],
         compiler_params=pltpu.CompilerParams(
-            collective_id=0, has_side_effects=True, vmem_limit_bytes=56 * 1024 * 1024
+            collective_id=0, has_side_effects=True, vmem_limit_bytes=(17 + n_cpl // 2) * 1024 * 1024
         ),
         cost_estimate=pl.CostEstimate(
             flops=2 * targets * slots * nodes * nodes * levels,

time: 42.4 us -> 42.8 us (level); the launches traced: 41.7 us -> 42.6 us
  local copies, waits for them, and re-layouts: 3.53 us -> 6.58 us
  Pallas kernels: 37.5 us -> 35.3 us
    unnamed x4 -> x12, local copies, waits for them, and re-layouts: 3.53 us -> 6.58 us
    pallas_call x1, Pallas kernels: 37.5 us -> 35.3 us  [local(): pl.pallas_call(functools.partial(kernel, n_cpl, n_mem), out_shape=(jax.Sh...]
where the time goes in v2:
time: 42.8 us; the launch traced here: 42.6 us
  Pallas kernels  35.3 us (82%)
  local copies, waits for them, and re-layouts  6.58 us (15%)
  between operations  0.65 us (2%)
    pallas_call x1, Pallas kernels, local(): pl.pallas_call(functools.partial(kernel, n_cpl, n_mem), out_shape=(jax.Sh...  35.3 us
    unnamed x12, local copies, waits for them, and re-layouts  6.58 us

profile of v2, /device:TPU:0, one launch (start us, length us, event | category | flops | bytes accessed | tf_op | source)
XLA Modules:
  0.0 42.6 jit_solution(12985303185185602035)
XLA Ops:
  0.6 0.0 copy-start
  0.6 1.6 %copy-done = bf16[8,8,128,128]{3,2,1,0:T(8,128)(2,1)S(1)} copy-done((bf16[8,8,128,128]{3,2,1,0:T(8,128)(2,1)S(1)}, bf16[8,8,128,128]{3,2,1,0:T(8,128)(2,1)}, u32[]{:S(2)}) %copy-start) | copy-done | bytes 2097176
  2.2 0.0 copy-start.1
  2.2 1.0 %copy-done.1 = bf16[2,128,1,720]{1,3,2,0:T(8,128)(2,1)S(1)} copy-done((bf16[2,128,1,720]{1,3,2,0:T(8,128)(2,1)S(1)}, bf16[2,128,1,720]{1,3,2,0:T(8,128)(2,1)}, u32[]{:S(2)}) %copy-start.1) | copy-done | bytes 368664
  3.2 0.0 copy-start.2
  3.2 0.7 %copy-done.2 = s32[8,8]{1,0:T(8,128)S(1)} copy-done((s32[8,8]{1,0:T(8,128)S(1)}, s32[8,8]{1,0:T(8,128)}, u32[]{:S(2)}) %copy-start.2) | copy-done | bytes 280
  3.9 0.0 copy-start.3
  3.9 0.7 %copy-done.3 = s32[4,4]{1,0:T(4,128)S(1)} copy-done((s32[4,4]{1,0:T(4,128)S(1)}, s32[4,4]{1,0:T(4,128)}, u32[]{:S(2)}) %copy-start.3) | copy-done | bytes 88
  4.6 0.0 copy-start.4
  4.6 0.7 %copy-done.4 = s32[8]{0:T(128)S(1)} copy-done((s32[8]{0:T(128)S(1)}, s32[8]{0:T(128)}, u32[]{:S(2)}) %copy-start.4) | copy-done | bytes 56
  5.2 35.3 %shard_map.68 = (bf16[8,720,128]{2,1,0:T(8,128)(2,1)S(1)}, f32[8,32,720]{2,1,0:T(8,128)S(1)}) custom-call(s32[8,8]{1,0:T(8,128)S(1)} %copy-done.2, s32[8]{0:T(128)S(1)} %copy-done.4, s32[4,4]{1,0:T(4,128)S(1)} %copy-done.3, bf16[2,720,128]{2,1,0:T(8,128)(2,1)S(1)} %bitcast.11, bf16[8,8,128,128]{3,2,1,0:T(8,128)(2,1)S(1)} %copy-done), custom_call_target="tpu_custom_call" | custom-call | flops 1509949440 | bytes 5046272 | tf_op jit(solution)/shard_map/pallas_call | solution.py:246
  40.6 1.1 %copy.11 = bf16[8,128,1,720]{1,3,2,0:T(8,128)(2,1)} copy(bf16[8,128,1,720]{1,3,2,0:T(8,128)(2,1)S(1)} %bitcast.10) | data formatting | bytes 2949120
  41.7 0.9 %copy.12 = f32[8,32,720]{2,1,0:T(8,128)} copy(f32[8,32,720]{2,1,0:T(8,128)S(1)} %get-tuple-element.11) | data formatting | bytes 1474560
Async XLA Ops:
  0.6 1.6 %copy-start = (bf16[8,8,128,128]{3,2,1,0:T(8,128)(2,1)S(1)}, bf16[8,8,128,128]{3,2,1,0:T(8,128)(2,1)}, u32[]{:S(2)}) copy-start(bf16[8,8,128,128]{3,2,1,0:T(8,128)(2,1)} %weights.1) | copy-start | bytes 6291460
  2.2 1.0 %copy-start.1 = (bf16[2,128,1,720]{1,3,2,0:T(8,128)(2,1)S(1)}, bf16[2,128,1,720]{1,3,2,0:T(8,128)(2,1)}, u32[]{:S(2)}) copy-start(bf16[2,128,1,720]{1,3,2,0:T(8,128)(2,1)} %param.5) | copy-start | bytes 1105924
  3.2 0.7 %copy-start.2 = (s32[8,8]{1,0:T(8,128)S(1)}, s32[8,8]{1,0:T(8,128)}, u32[]{:S(2)}) copy-start(s32[8,8]{1,0:T(8,128)} %cover_source.1) | copy-start | bytes 772
  3.9 0.7 %copy-start.3 = (s32[4,4]{1,0:T(4,128)S(1)}, s32[4,4]{1,0:T(4,128)}, u32[]{:S(2)}) copy-start(s32[4,4]{1,0:T(4,128)} %send_pick.1) | copy-start | bytes 196
  4.6 0.7 %copy-start.4 = (s32[8]{0:T(128)S(1)}, s32[8]{0:T(128)}, u32[]{:S(2)}) copy-start(s32[8]{0:T(128)} %cover_count.1) | copy-start | bytes 100

commit v3 on v2

--- a/solution.py
+++ b/solution.py
@@ -10,6 +10,7 @@
 MESH = pl.DeviceIdType.MESH
 WIDTH = 128
 AHEAD = 2
+STEPS = 32000.0
 GROUP = 4
 
 
@@ -34,11 +35,9 @@
     *rest,
 ):
     stages = n_mem.bit_length() - 1
-    totals = rest[:stages]
-    landed = rest[stages : 2 * stages]
-    pool_send, pool_recv, weight_sem, limited_sem, mean_sem = rest[2 * stages : 2 * stages + 5]
-    stage_send = rest[2 * stages + 5 : 3 * stages + 5]
-    stage_recv = rest[3 * stages + 5 : 4 * stages + 5]
+    halves, first_landed, *rest = rest
+    pool_send, pool_recv, weight_sem, limited_sem, mean_sem, half_send, half_recv, *rest = rest
+    later = [None] + [rest[9 * s : 9 * s + 9] for s in range(stages - 1)]
     targets, slots, nodes, _ = weights.shape
     levels = sources.shape[1]
     pieces = pl.cdiv(levels, WIDTH)
@@ -106,16 +105,40 @@
     flipped[n_cpl] = jnp.zeros(flipped.shape[1:], flipped.dtype)
     weight_copy.wait()
 
-    def stage_copy(s, piece, group):
-        spot = (piece, group)
+    def half_copy(piece, group):
         return pltpu.make_async_remote_copy(
-            src_ref=totals[s].at[spot + (1 - bits[s],)],
-            dst_ref=landed[s].at[spot],
-            send_sem=stage_send[s].at[spot],
-            recv_sem=stage_recv[s].at[spot],
-            device_id={"mem": partners[s]},
+            src_ref=halves.at[piece, group, 1 - bits[0]],
+            dst_ref=first_landed.at[piece, group],
+            send_sem=half_send.at[piece, group],
+            recv_sem=half_recv.at[piece, group],
+            device_id={"mem": partners[0]},
             device_id_type=MESH,
         )
+
+    def later_copies(s, piece, group):
+        _, codes, codes_in, peaks, peaks_in, *sems = later[s]
+        return [
+            pltpu.make_async_remote_copy(
+                src_ref=source.at[piece, group],
+                dst_ref=target.at[piece, group],
+                send_sem=send_sem.at[piece, group],
+                recv_sem=recv_sem.at[piece, group],
+                device_id={"mem": partners[s]},
+                device_id_type=MESH,
+            )
+            for source, target, send_sem, recv_sem in (
+                (codes, codes_in, sems[0], sems[1]),
+                (peaks, peaks_in, sems[2], sems[3]),
+            )
+        ]
+
+    def combined(s, piece, group, q):
+        if s == 1:
+            return halves[piece, group, bits[0], q] + first_landed[piece, group, q]
+        kept, _, codes_in, _, peaks_in, *_ = later[s - 1]
+        arrived = codes_in[piece, group, q].astype(jnp.int32).astype(jnp.float32)
+        scale = peaks_in[piece, group] * (1.0 / STEPS)
+        return kept[piece, group, q] + arrived * scale[:, None, :]
 
     def remap(piece, target):
         start, size = rows_of(piece)
@@ -162,11 +185,12 @@
         )
 
     def collect(piece):
-        last = stages - 1
         start, size = rows_of(piece)
         for group in range(groups):
-            stage_copy(last, piece, group).wait_recv()
-            total = totals[last][piece, group, bits[last], 0] + landed[last][piece, group, 0]
+            if stages > 1:
+                for copy in later_copies(stages - 1, piece, group):
+                    copy.wait_recv()
+            total = combined(stages, piece, group, 0)
             mean_out[pl.ds(group * GROUP, GROUP), :, pl.ds(start, size)] = (
                 total * (1.0 / n_mem)
             )[:, :, :size]
@@ -195,18 +219,34 @@
             for one in range(GROUP):
                 limited = remap(piece, group * GROUP + one)
                 for q in range(n_mem):
-                    totals[0][piece, group, q % 2, q // 2, one] = limited[q * share : (q + 1) * share]
-            stage_copy(0, piece, group).start()
+                    halves[piece, group, q % 2, q // 2, one] = limited[q * share : (q + 1) * share]
+            half_copy(piece, group).start()
 
         limited_copy(piece).start()
         for s in range(1, stages):
             for group in range(groups):
-                stage_copy(s - 1, piece, group).wait_recv()
-                for q in range(n_mem >> s):
-                    totals[s][piece, group, q % 2, q // 2] = (
-                        totals[s - 1][piece, group, bits[s - 1], q] + landed[s - 1][piece, group, q]
+                if s == 1:
+                    half_copy(piece, group).wait_recv()
+                else:
+                    for copy in later_copies(s - 1, piece, group):
+                        copy.wait_recv()
+                kept, codes, _, peaks, *_ = later[s]
+                parts = range((n_mem >> s) // 2)
+                going = [combined(s, piece, group, 2 * q + 1 - bits[s]) for q in parts]
+                peak = functools.reduce(
+                    jnp.maximum, [jnp.max(jnp.abs(one), axis=1) for one in going]
+                )
+                peak = jnp.maximum(peak, 1e-30)
+                peaks[piece, group] = peak
+                factor = (STEPS / peak)[:, None, :]
+                for q in parts:
+                    codes[piece, group, q] = (
+                        jnp.round(going[q] * factor).astype(jnp.int32).astype(jnp.int16)
                     )
-                stage_copy(s, piece, group).start()
+                for copy in later_copies(s, piece, group):
+                    copy.start()
+                for q in parts:
+                    kept[piece, group, q] = combined(s, piece, group, 2 * q + bits[s])
         if piece > 0:
             collect(piece - 1)
     collect(pieces - 1)
@@ -218,8 +258,10 @@
             pool_copy(piece, distance, me).wait_send()
 
         for group in range(groups):
-            for s in range(stages):
-                stage_copy(s, piece, group).wait_send()
+            half_copy(piece, group).wait_send()
+            for s in range(1, stages):
+                for copy in later_copies(s, piece, group):
+                    copy.wait_send()
         limited_copy(piece).wait()
         mean_copy(piece).wait()
 
@@ -233,23 +275,32 @@
     share = nodes // n_mem
     stages = n_mem.bit_length() - 1
     turned = jnp.transpose(sources, (0, 2, 3, 1)).reshape(blocks, levels, nodes)
-    totals, landed, sems = [], [], []
-    for s in range(stages):
-        half = (n_mem >> s) // 2
-        lead = (pieces, groups)
-        totals.append(pltpu.VMEM(lead + (2, half, GROUP, share, WIDTH), jnp.float32))
-        landed.append(pltpu.VMEM(lead + (half, GROUP, share, WIDTH), jnp.float32))
-        sems.append(pltpu.SemaphoreType.DMA(lead))
+    lead = (pieces, groups)
+    pairs = pltpu.SemaphoreType.DMA(lead)
+    half = lead + (n_mem // 2, GROUP, share, WIDTH)
+    halves = pltpu.VMEM(lead + (2, n_mem // 2, GROUP, share, WIDTH), jnp.float32)
+    later = []
+    for s in range(1, stages):
+        part = lead + ((n_mem >> s) // 2, GROUP, share, WIDTH)
+        peak = pltpu.VMEM(lead + (GROUP, WIDTH), jnp.float32)
+        later += [
+            pltpu.VMEM(part, jnp.float32),
+            pltpu.VMEM(part, jnp.int16),
+            pltpu.VMEM(part, jnp.int16),
+            peak,
+            peak,
+            *[pairs] * 4,
+        ]
     vmem = pl.BlockSpec(memory_space=pltpu.VMEM)
     whole = pl.BlockSpec(memory_space=pl.ANY)
     smem = pl.BlockSpec(memory_space=pltpu.SMEM)
     remapped, ens_mean = pl.pallas_call(
         functools.partial(kernel, n_cpl, n_mem),
         out_shape=(
-            jax.ShapeDtypeStruct((targets, levels, nodes), jnp.bfloat16),
-            jax.ShapeDtypeStruct((targets, share, levels), jnp.float32),
+            pltpu.VMEM((targets, levels, nodes), jnp.bfloat16),
+            pltpu.VMEM((targets, share, levels), jnp.float32),
         ),
-        in_specs=[smem, smem, smem, vmem, pl.BlockSpec(memory_space=pltpu.HBM)],
+        in_specs=[smem, smem, smem, vmem, whole],
         out_specs=(whole, whole),
         scratch_shapes=[
             pltpu.VMEM((n_cpl - 1, levels, nodes), jnp.bfloat16),
@@ -260,18 +311,19 @@
             pltpu.VMEM((targets, slots, nodes, nodes), jnp.bfloat16),
             pltpu.VMEM((targets, levels, nodes), jnp.bfloat16),
             pltpu.VMEM((targets, share, levels), jnp.float32),
-            *totals,
-            *landed,
+            halves,
+            pltpu.VMEM(half, jnp.float32),
             pltpu.SemaphoreType.DMA((pieces, n_cpl - 1)),
             pltpu.SemaphoreType.DMA((pieces, n_cpl - 1)),
             pltpu.SemaphoreType.DMA,
             pltpu.SemaphoreType.DMA((pieces,)),
             pltpu.SemaphoreType.DMA((pieces,)),
-            *sems,
-            *sems,
+            pairs,
+            pairs,
+            *later,
         ],
         compiler_params=pltpu.CompilerParams(
-            collective_id=0, has_side_effects=True, vmem_limit_bytes=(17 + n_cpl // 2) * 1024 * 1024
+            collective_id=0, has_side_effects=True, vmem_limit_bytes=56 * 1024 * 1024
         ),
         cost_estimate=pl.CostEstimate(
             flops=2 * targets * slots * nodes * nodes * levels,

time: 42.8 us -> 34.7 us (0.81)
  local copies, waits for them, and re-layouts: 6.58 us -> 1.99 us
  Pallas kernels: 35.3 us -> 31.9 us
    unnamed x12 -> x2, local copies, waits for them, and re-layouts: 6.58 us -> 1.99 us
    pallas_call x1, Pallas kernels: 35.3 us -> 31.9 us  [local(): pl.pallas_call(functools.partial(kernel, n_cpl, n_mem), out_shape=(pltpu....]
where the time goes in v3:
time: 34.7 us; the launch traced here: 34.5 us
  Pallas kernels  31.9 us (92%)
  local copies, waits for them, and re-layouts  1.99 us (6%)
  between operations  0.64 us (2%)
    pallas_call x1, Pallas kernels, local(): pl.pallas_call(functools.partial(kernel, n_cpl, n_mem), out_shape=(pltpu....  31.9 us
    unnamed x2, local copies, waits for them, and re-layouts  1.99 us

profile of v3, /device:TPU:0, one launch (start us, length us, event | category | flops | bytes accessed | tf_op | source)
XLA Modules:
  0.0 34.5 jit_solution(9562619559242998665)
XLA Ops:
  0.6 31.9 %shard_map.68 = (bf16[8,720,128]{2,1,0:T(8,128)(2,1)S(1)}, f32[8,32,720]{2,1,0:T(8,128)S(1)}) custom-call(s32[8,8]{1,0:T(8,128)} %cover_source.1, s32[8]{0:T(128)} %cover_count.1, s32[4,4]{1,0:T(4,128)} %send_pick.1, bf16[2,720,128]{2,1,0:T(8,128)(2,1)} %bitcast.11, bf16[8,8,128,128]{3,2,1,0:T(8,128)(2,1)} %weights.1), custom_call_target="tpu_custom_call" | custom-call | flops 1509949440 | bytes 5046272 | tf_op jit(solution)/shard_map/pallas_call | solution.py:297
  32.5 1.1 %copy.11 = bf16[8,128,1,720]{1,3,2,0:T(8,128)(2,1)} copy(bf16[8,128,1,720]{1,3,2,0:T(8,128)(2,1)S(1)} %bitcast.10) | data formatting | bytes 2949120
  33.6 0.9 %copy.12 = f32[8,32,720]{2,1,0:T(8,128)} copy(f32[8,32,720]{2,1,0:T(8,128)S(1)} %get-tuple-element.9) | data formatting | bytes 1474560

commit v4 on v3

--- a/solution.py
+++ b/solution.py
@@ -30,13 +30,11 @@
     low,
     high,
     held,
-    limited_out,
-    mean_out,
     *rest,
 ):
     stages = n_mem.bit_length() - 1
     halves, first_landed, *rest = rest
-    pool_send, pool_recv, weight_sem, limited_sem, mean_sem, half_send, half_recv, *rest = rest
+    pool_send, pool_recv, weight_sem, half_send, half_recv, *rest = rest
     later = [None] + [rest[9 * s : 9 * s + 9] for s in range(stages - 1)]
     targets, slots, nodes, _ = weights.shape
     levels = sources.shape[1]
@@ -165,24 +163,8 @@
         factor = jnp.clip(jnp.minimum(rising, falling), 0.0, 1.0)
         limited = center + factor * (summed - center)
         turned = limited.astype(jnp.bfloat16).T
-        limited_out[target, pl.ds(start, size)] = turned[:size]
+        remapped[target, pl.ds(start, size)] = turned[:size]
         return limited
-
-    def limited_copy(piece):
-        start, size = rows_of(piece)
-        return pltpu.make_async_copy(
-            limited_out.at[:, pl.ds(start, size)],
-            remapped.at[:, pl.ds(start, size)],
-            limited_sem.at[piece],
-        )
-
-    def mean_copy(piece):
-        start, size = rows_of(piece)
-        return pltpu.make_async_copy(
-            mean_out.at[:, :, pl.ds(start, size)],
-            ens_mean.at[:, :, pl.ds(start, size)],
-            mean_sem.at[piece],
-        )
 
     def collect(piece):
         start, size = rows_of(piece)
@@ -191,10 +173,9 @@
                 for copy in later_copies(stages - 1, piece, group):
                     copy.wait_recv()
             total = combined(stages, piece, group, 0)
-            mean_out[pl.ds(group * GROUP, GROUP), :, pl.ds(start, size)] = (
+            ens_mean[pl.ds(group * GROUP, GROUP), :, pl.ds(start, size)] = (
                 total * (1.0 / n_mem)
             )[:, :, :size]
-        mean_copy(piece).start()
 
     for piece in range(pieces):
         start, size = rows_of(piece)
@@ -206,7 +187,7 @@
         if piece + AHEAD < pieces:
             send(piece + AHEAD)
 
-        @pl.loop(0, n_cpl)
+        @pl.loop(0, n_cpl, unroll=n_cpl <= 4)
         def _(block):
             values = pool[block, pl.ds(piece * WIDTH, WIDTH)].T
             flipped[block] = values
@@ -214,15 +195,13 @@
             low[block] = jnp.min(wide, axis=0, keepdims=True)
             high[block] = jnp.max(wide, axis=0, keepdims=True)
 
-        @pl.loop(0, groups)
-        def _(group):
+        for group in range(groups):
             for one in range(GROUP):
                 limited = remap(piece, group * GROUP + one)
                 for q in range(n_mem):
                     halves[piece, group, q % 2, q // 2, one] = limited[q * share : (q + 1) * share]
             half_copy(piece, group).start()
 
-        limited_copy(piece).start()
         for s in range(1, stages):
             for group in range(groups):
                 if s == 1:
@@ -262,8 +241,6 @@
             for s in range(1, stages):
                 for copy in later_copies(s, piece, group):
                     copy.wait_send()
-        limited_copy(piece).wait()
-        mean_copy(piece).wait()
 
 
 def local(n_cpl, n_mem, sources, weights, cover_source, cover_count, send_pick):
@@ -301,7 +278,7 @@
             pltpu.VMEM((targets, share, levels), jnp.float32),
         ),
         in_specs=[smem, smem, smem, vmem, whole],
-        out_specs=(whole, whole),
+        out_specs=(vmem, vmem),
         scratch_shapes=[
             pltpu.VMEM((n_cpl - 1, levels, nodes), jnp.bfloat16),
             pltpu.VMEM((n_cpl, padded, nodes), jnp.bfloat16),
@@ -309,15 +286,11 @@
             pltpu.VMEM((n_cpl, 1, WIDTH), jnp.float32),
             pltpu.VMEM((n_cpl, 1, WIDTH), jnp.float32),
             pltpu.VMEM((targets, slots, nodes, nodes), jnp.bfloat16),
-            pltpu.VMEM((targets, levels, nodes), jnp.bfloat16),
-            pltpu.VMEM((targets, share, levels), jnp.float32),
             halves,
             pltpu.VMEM(half, jnp.float32),
             pltpu.SemaphoreType.DMA((pieces, n_cpl - 1)),
             pltpu.SemaphoreType.DMA((pieces, n_cpl - 1)),
             pltpu.SemaphoreType.DMA,
-            pltpu.SemaphoreType.DMA((pieces,)),
-            pltpu.SemaphoreType.DMA((pieces,)),
             pairs,
             pairs,
             *later,

time: 34.7 us -> 33.8 us (0.974)
  Pallas kernels: 31.9 us -> 31 us
    pallas_call x1, Pallas kernels: 31.9 us -> 31 us  [local(): pl.pallas_call(functools.partial(kernel, n_cpl, n_mem), out_shape=(pltpu....]
where the time goes in v4:
time: 33.8 us; the launch traced here: 33.7 us
  Pallas kernels  31 us (92%)
  local copies, waits for them, and re-layouts  1.99 us (6%)
  between operations  0.64 us (2%)
    pallas_call x1, Pallas kernels, local(): pl.pallas_call(functools.partial(kernel, n_cpl, n_mem), out_shape=(pltpu....  31 us
    unnamed x2, local copies, waits for them, and re-layouts  1.99 us

profile of v4, /device:TPU:0, one launch (start us, length us, event | category | flops | bytes accessed | tf_op | source)
XLA Modules:
  0.0 33.7 jit_solution(3157757864931214985)
XLA Ops:
  0.6 31.0 %shard_map.68 = (bf16[8,720,128]{2,1,0:T(8,128)(2,1)S(1)}, f32[8,32,720]{2,1,0:T(8,128)S(1)}) custom-call(s32[8,8]{1,0:T(8,128)} %cover_source.1, s32[8]{0:T(128)} %cover_count.1, s32[4,4]{1,0:T(4,128)} %send_pick.1, bf16[2,720,128]{2,1,0:T(8,128)(2,1)} %bitcast.11, bf16[8,8,128,128]{3,2,1,0:T(8,128)(2,1)} %weights.1), custom_call_target="tpu_custom_call" | custom-call | flops 1509949440 | bytes 5046272 | tf_op jit(solution)/shard_map/pallas_call | solution.py:274
  31.7 1.1 %copy.11 = bf16[8,128,1,720]{1,3,2,0:T(8,128)(2,1)} copy(bf16[8,128,1,720]{1,3,2,0:T(8,128)(2,1)S(1)} %bitcast.10) | data formatting | bytes 2949120
  32.8 0.9 %copy.12 = f32[8,32,720]{2,1,0:T(8,128)} copy(f32[8,32,720]{2,1,0:T(8,128)S(1)} %get-tuple-element.9) | data formatting | bytes 1474560

commit v5 on v4

--- a/solution.py
+++ b/solution.py
@@ -85,7 +85,7 @@
     def send(piece):
         @pl.loop(1, n_cpl)
         def _(distance):
-            pool_copy(piece, distance, me).start()
+            pool_copy(piece, 1 + lax.rem(distance + n_cpl // 2 - 2, n_cpl - 1), me).start()
 
     fill(0)
     pl.semaphore_wait(barrier, n_cpl - 1 + stages)

time: 33.8 us -> 34.8 us (1.030)
  Pallas kernels: 31 us -> 32 us
    pallas_call x1, Pallas kernels: 31 us -> 32 us  [local(): pl.pallas_call(functools.partial(kernel, n_cpl, n_mem), out_shape=(pltpu....]
where the time goes in v5:
time: 34.8 us; the launch traced here: 34.7 us
  Pallas kernels  32 us (92%)
  local copies, waits for them, and re-layouts  1.99 us (6%)
  between operations  0.64 us (2%)
    pallas_call x1, Pallas kernels, local(): pl.pallas_call(functools.partial(kernel, n_cpl, n_mem), out_shape=(pltpu....  32 us
    unnamed x2, local copies, waits for them, and re-layouts  1.99 us

profile of v5, /device:TPU:0, one launch (start us, length us, event | category | flops | bytes accessed | tf_op | source)
XLA Modules:
  0.0 34.7 jit_solution(13254045998987326578)
XLA Ops:
  0.6 32.0 %shard_map.68 = (bf16[8,720,128]{2,1,0:T(8,128)(2,1)S(1)}, f32[8,32,720]{2,1,0:T(8,128)S(1)}) custom-call(s32[8,8]{1,0:T(8,128)} %cover_source.1, s32[8]{0:T(128)} %cover_count.1, s32[4,4]{1,0:T(4,128)} %send_pick.1, bf16[2,720,128]{2,1,0:T(8,128)(2,1)} %bitcast.11, bf16[8,8,128,128]{3,2,1,0:T(8,128)(2,1)} %weights.1), custom_call_target="tpu_custom_call" | custom-call | flops 1509949440 | bytes 5046272 | tf_op jit(solution)/shard_map/pallas_call | solution.py:274
  32.7 1.1 %copy.11 = bf16[8,128,1,720]{1,3,2,0:T(8,128)(2,1)} copy(bf16[8,128,1,720]{1,3,2,0:T(8,128)(2,1)S(1)} %bitcast.10) | data formatting | bytes 2949120
  33.8 0.9 %copy.12 = f32[8,32,720]{2,1,0:T(8,128)} copy(f32[8,32,720]{2,1,0:T(8,128)S(1)} %get-tuple-element.9) | data formatting | bytes 1474560
